TPU v7x, 256 devices: a whole 4x4x8 slice. The times are simulated.
256 devices in a mesh: rows: 32 (over z_hi, y, x), cols: 8 (over z_lo, core).
Axes of the slice: x: 4, y: 4, z: 8 (z_hi: 2, z_lo: 4; z = z_hi * 4 + z_lo), core: 2. Of those that a mesh axis runs over, the one named last changes fastest.
Arguments:
- logged: bfloat16 [32768, 256], P(('rows', 'cols')), may hold values from -8 to 8
- fresh: bfloat16 [65536, 256], P(('cols', 'rows')), may hold values from -6 to 6
- warm: float32 [65536], P('cols'), may hold values from -1 to 1
Outputs:
- row_potential: float32 [32768], P('rows')
- col_potential: float32 [65536], P('cols')
- reward: float32 [32768], P('rows')
All inputs are finite; a program needn't handle non-finite values.
Results may differ from a plain program's by a relative error of at most 0.0013.
Values may be sent and summed in bfloat16 or wider, within the bound.
No kernel may reach another device: no remote copies, remote signals or barrier semaphores. Data moves between devices by JAX's collectives and lax.ppermute only.
A program may use at most 128 MiB of HBM per device.

v0:
```python
import jax
import jax.numpy as jnp
from jax import lax
from jax.sharding import PartitionSpec as P

EPS = 0.01


def body(logged, fresh, warm):
    block = lax.all_gather(logged, "cols", axis=0, tiled=True)
    wide = block.astype(jnp.float32)
    block_sq = jnp.sum(wide * wide, axis=1)
    width = block.shape[1]
    total_rows = block.shape[0] * lax.axis_size("rows")
    total_cols = warm.shape[0] * lax.axis_size("cols")
    piece = lax.all_gather(fresh, "rows", axis=0, tiled=True)
    piece_wide = piece.astype(jnp.float32)
    piece_sq = jnp.sum(piece_wide * piece_wide, axis=1)
    inner = lax.dot_general(
        block, piece, (((1,), (1,)), ((), ())), preferred_element_type=jnp.float32
    )
    stored = (block_sq[:, None] + piece_sq[None, :] - 2.0 * inner) / width

    def get_tile():
        return stored

    expo = (warm[None, :] - get_tile()) / EPS
    top = jnp.max(expo, axis=1)
    total = jnp.sum(jnp.exp(expo - top[:, None]), axis=1)
    both = lax.pmax(top, "cols")
    total = lax.psum(total * jnp.exp(top - both), "cols")
    top = both
    row_potential = -EPS * (top + jnp.log(total)) - EPS * jnp.log(jnp.float32(total_rows))
    expo = (row_potential[:, None] - get_tile()) / EPS
    top = jnp.max(expo, axis=0)
    total = jnp.sum(jnp.exp(expo - top[None, :]), axis=0)
    both = lax.pmax(top.astype(jnp.bfloat16), "rows").astype(top.dtype)
    total = lax.psum(total * jnp.exp(top - both), "rows")
    top = both
    col_potential = -EPS * (top + jnp.log(total)) - EPS * jnp.log(jnp.float32(total_cols))
    cost = get_tile()
    plan = jnp.exp((row_potential[:, None] + col_potential[None, :] - cost) / EPS)
    partial_cost = jnp.sum(plan * cost, axis=1)
    reward = -jnp.float32(total_rows) * lax.psum(partial_cost, "cols")
    return (row_potential, col_potential, reward)


def solution(mesh):
    return jax.shard_map(
        body,
        mesh=mesh,
        in_specs=(P(("rows", "cols"), None), P(("cols", "rows"), None), P("cols")),
        out_specs=(P("rows"), P("cols"), P("rows")),
        check_vma=False,
    )
```

profile of v0, /device:TPU:1, one launch (start us, length us, event | category | flops | bytes accessed | tf_op | source)
XLA Modules:
  0.0 682.2 jit_solution(6621677491578648344)
XLA Ops:
  7.2 0.0 all-gather.2.cloned.1.call-start
  7.2 0.7 all-gather.2.cloned.1.call-update
  7.9 18.0 %all_gather.6 = bf16[1024,256]{1,0:T(8,128)(2,1)S(1)} all-gather(bf16[128,256]{1,0:T(8,128)(2,1)} %param.3), channel_id=1, replica_groups=mesh['rows'=32,'cols'=8] {'cols'}, dimensions={0}, use_global_device_ids=true | all-gather | bytes 589824 | tf_op jit(solution)/shard_map/all_gather | solution.py:10
  25.9 0.2 multiply_reduce_fusion.2
  26.1 96.6 %all-gather.2.cloned.1.call-done = bf16[8192,256]{1,0:T(8,128)(2,1)} async-done(((bf16[256,256]{1,0:T(8,128)(2,1)}), bf16[8192,256]{1,0:T(8,128)(2,1)}) %all-gather.2.cloned.1.call-update) | async-done | bytes 4194320 | tf_op jit(solution)/shard_map/all_gather | solution.py:16
  122.7 3.3 multiply_reduce_fusion.1
  126.0 0.0 copy-start.2
  126.1 15.9 %fusion = (f32[1024]{0:T(1024)S(1)}, f32[1024,8192]{1,0:T(8,128)}) fusion(f32[8192]{0:T(1024)} %param.5, bf16[1024,256]{1,0:T(8,128)(2,1)S(1)} %all_gather.6, bf16[8192,256]{1,0:T(8,128)(2,1)} %all-gather.2.cloned.1.call-done, f32[8192]{0:T(1024)S(1)} %multiply_reduce_fusion.1, f32[1024]{0:T(1024)S(1)} %multiply_reduce_fusion.2), kind=kOutput, calls=%fused_computation.6 | convolution fusion | flops 4353686528 | bytes 38346752 | tf_op jit(solution)/shard_map/dot_general | solution.py:19
  142.0 17.9 %pmax.14 = f32[1024]{0:T(1024)S(1)} all-reduce(f32[1024]{0:T(1024)S(1)} %get-tuple-element.3), channel_id=1, replica_groups=mesh['rows'=32,'cols'=8] {'cols'}, use_global_device_ids=true, to_apply=%region_3.0 | all-reduce | flops 1024 | bytes 8192 | tf_op jit(solution)/shard_map/pmax | solution.py:30
  159.9 0.0 copy-done.2
  159.9 14.7 %exponential_reduce_fusion.1 = f32[1024]{0:T(1024)S(1)} fusion(f32[1024,8192]{1,0:T(8,128)} %get-tuple-element.4, f32[1024]{0:T(1024)S(1)} %get-tuple-element.3, f32[8192]{0:T(1024)S(1)} %copy-done.2), kind=kLoop, calls=%fused_computation.3 | loop fusion | flops 33553408 | bytes 33595392 | tf_op jit(solution)/shard_map/reduce_sum | solution.py:29
  174.7 13.6 %psum.21 = f32[1024]{0:T(1024)S(1)} all-reduce(f32[1024]{0:T(1024)S(1)} %exponential_multiply_fusion), channel_id=1, replica_groups=mesh['rows'=32,'cols'=8] {'cols'}, use_global_device_ids=true, to_apply=%region_5.0 | all-reduce | flops 1024 | bytes 8192 | tf_op jit(solution)/shard_map/psum | solution.py:31
  188.3 0.0 copy-start.1
  188.3 12.9 %fusion.1 = f32[8192]{0:T(1024)S(1)} fusion(f32[1024,8192]{1,0:T(8,128)} %get-tuple-element.4, f32[1024]{0:T(1024)S(1)} %multiply_add_fusion), kind=kLoop, calls=%fused_computation.7 | loop fusion | flops 25157632 | bytes 33591296 | tf_op jit(solution)/shard_map/reduce_max | solution.py:35
  201.2 14.5 %exponential_reduce_fusion = f32[8192]{0:T(1024)S(1)} fusion(f32[1024,8192]{1,0:T(8,128)} %get-tuple-element.4, f32[8192]{0:T(1024)S(1)} %fusion.1, f32[1024]{0:T(1024)S(1)} %multiply_add_fusion), kind=kLoop, calls=%fused_computation.1 | loop fusion | flops 33546240 | bytes 33624064 | tf_op jit(solution)/shard_map/reduce_sum | solution.py:36
  215.7 187.5 %pmax.15 = bf16[8192]{0:T(1024)(128)(2,1)S(1)} all-reduce(bf16[8192]{0:T(1024)(128)(2,1)S(1)} %convert_element_type.14), channel_id=1, replica_groups=mesh['rows'=32,'cols'=8] {'rows'}, use_global_device_ids=true, to_apply=%region_7.0 | all-reduce | flops 8192 | bytes 32768 | tf_op jit(solution)/shard_map/pmax | solution.py:37
  403.2 187.1 %psum.22 = f32[8192]{0:T(1024)S(1)} all-reduce(f32[8192]{0:T(1024)S(1)} %fusion.3), channel_id=1, replica_groups=mesh['rows'=32,'cols'=8] {'rows'}, use_global_device_ids=true, to_apply=%region_9.0 | all-reduce | flops 8192 | bytes 65536 | tf_op jit(solution)/shard_map/psum | solution.py:38
  590.4 0.0 copy-done.1
  590.4 0.0 copy-start
  590.4 15.1 %multiply_reduce_fusion = f32[1024]{0:T(1024)S(1)} fusion(f32[1024,8192]{1,0:T(8,128)} %get-tuple-element.4, f32[8192]{0:T(1024)S(1)} %fusion.5, f32[1024]{0:T(1024)S(1)} %multiply_add_fusion), kind=kLoop, calls=%fused_computation | loop fusion | flops 41942016 | bytes 33595392 | tf_op jit(solution)/shard_map/reduce_sum | solution.py:43
  605.5 69.3 %psum.23 = f32[1024]{0:T(1024)S(1)} all-reduce(f32[1024]{0:T(1024)S(1)} %multiply_reduce_fusion), channel_id=1, replica_groups=mesh['rows'=32,'cols'=8] {'cols'}, use_global_device_ids=true, to_apply=%region_11.0 | all-reduce | flops 1024 | bytes 8192 | tf_op jit(solution)/shard_map/psum | solution.py:44
  674.7 0.6 broadcast_multiply_fusion
  675.3 0.0 copy-done
  (5 shorter events, 0.1 us)
Async XLA Ops:
  7.2 115.5 %all-gather.2.cloned.1.call-start = ((), (), s32[]{:S(2)}) async-start(), calls=%async_computation | async-start | bytes 4325376 | tf_op jit(solution)/shard_map/all_gather | solution.py:16
  126.0 33.9 %copy-start.2 = (f32[8192]{0:T(1024)S(1)}, f32[8192]{0:T(1024)}, u32[]{:S(2)}) copy-start(f32[8192]{0:T(1024)} %param.5) | copy-start | bytes 98308
  188.3 402.1 %copy-start.1 = (f32[1024]{0:T(1024)}, f32[1024]{0:T(1024)S(1)}, u32[]{:S(2)}) copy-start(f32[1024]{0:T(1024)S(1)} %multiply_add_fusion) | copy-start | bytes 12292
  590.4 85.0 %copy-start = (f32[8192]{0:T(1024)}, f32[8192]{0:T(1024)S(1)}, u32[]{:S(2)}) copy-start(f32[8192]{0:T(1024)S(1)} %fusion.5) | copy-start | bytes 98308
Sparse Core Ops, SparseCore 0:
  11.4 111.2 all-gather.1
where the time goes:
time: 683 us; the launch traced here: 682 us
  blocking collectives  493 us (72%)
  waiting for transfers between devices  97.3 us (14%)
  other arithmetic  61.4 us (9%)
  matrix products  15.9 us (2%)
  between operations  14.1 us (2%)
    pmax x1, blocking collectives, body(): both = lax.pmax(top.astype(jnp.bfloat16), 'rows').astype(top.dtype)  188 us
    psum x1, blocking collectives, body(): total = lax.psum(total * jnp.exp(top - both), 'rows')  187 us
    all_gather x1, waiting for transfers between devices, body(): piece = lax.all_gather(fresh, 'rows', axis=0, tiled=True)  96.6 us
    psum x1, blocking collectives, body(): reward = -jnp.float32(total_rows) * lax.psum(partial_cost, 'cols')  69.3 us
    all_gather x1, blocking collectives, body(): block = lax.all_gather(logged, 'cols', axis=0, tiled=True)  18 us
    pmax x1, blocking collectives, body(): both = lax.pmax(top, 'cols')  17.9 us
    dot_general x1, matrix products, body(): lax.dot_general(block, piece, (((1,), (1,)), ((), ())), preferred_element...  15.9 us
    reduce_sum x1, other arithmetic, body(): partial_cost = jnp.sum(plan * cost, axis=1)  15.1 us
  transfers between devices with their start and end apart: 1, of which 1 were waited for; matrix products, arithmetic and copies ran while one was open for 0% of the time, Pallas kernels for 0%

commit v1 on v0

--- a/solution.py
+++ b/solution.py
@@ -35,7 +35,7 @@
     top = jnp.max(expo, axis=0)
     total = jnp.sum(jnp.exp(expo - top[None, :]), axis=0)
     both = lax.pmax(top.astype(jnp.bfloat16), "rows").astype(top.dtype)
-    total = lax.psum(total * jnp.exp(top - both), "rows")
+    total = jnp.sum(lax.all_gather(total * jnp.exp(top - both), "rows"), axis=0)
     top = both
     col_potential = -EPS * (top + jnp.log(total)) - EPS * jnp.log(jnp.float32(total_cols))
     cost = get_tile()

time: 683 us -> 550 us (0.81)
  blocking collectives: 493 us -> 252 us
  waiting for transfers between devices: 97.3 us -> 203 us
    psum x1 -> x0, blocking collectives: 187 us -> none  [body(): total = lax.psum(total * jnp.exp(top - both), 'rows')]
    all_gather x0 -> x1, waiting for transfers between devices: none -> 106 us  [body(): total = jnp.sum(lax.all_gather(total * jnp.exp(top - both), 'rows'), axis=0)]
    psum x1, blocking collectives: 69.3 us -> 15.2 us  [body(): reward = -jnp.float32(total_rows) * lax.psum(partial_cost, 'cols')]
  transfers between devices with their start and end apart: 1 -> 2, of which waited for: 1 -> 2; matrix products, arithmetic and copies ran while one was open for 0% -> 0% of each run, Pallas kernels for 0% -> 0%
where the time goes in v1:
time: 550 us; the launch traced here: 549 us
  blocking collectives  252 us (46%)
  waiting for transfers between devices  203 us (37%)
  other arithmetic  62.1 us (11%)
  matrix products  15.9 us (3%)
  between operations  14.1 us (3%)
    pmax x1, blocking collectives, body(): both = lax.pmax(top.astype(jnp.bfloat16), 'rows').astype(top.dtype)  188 us
    all_gather x1, waiting for transfers between devices, body(): total = jnp.sum(lax.all_gather(total * jnp.exp(top - both), 'rows'), axis=0)  106 us
    all_gather x1, waiting for transfers between devices, body(): piece = lax.all_gather(fresh, 'rows', axis=0, tiled=True)  96.6 us
    all_gather x1, blocking collectives, body(): block = lax.all_gather(logged, 'cols', axis=0, tiled=True)  18 us
    pmax x1, blocking collectives, body(): both = lax.pmax(top, 'cols')  17.9 us
    dot_general x1, matrix products, body(): lax.dot_general(block, piece, (((1,), (1,)), ((), ())), preferred_element...  15.9 us
    psum x1, blocking collectives, body(): reward = -jnp.float32(total_rows) * lax.psum(partial_cost, 'cols')  15.2 us
    reduce_sum x1, other arithmetic, body(): partial_cost = jnp.sum(plan * cost, axis=1)  15.1 us
  transfers between devices with their start and end apart: 2, of which 2 were waited for; matrix products, arithmetic and copies ran while one was open for 0% of the time, Pallas kernels for 0%

profile of v1, /device:TPU:1, one launch (start us, length us, event | category | flops | bytes accessed | tf_op | source)
XLA Modules:
  0.0 549.4 jit_solution(879036243989912328)
XLA Ops:
  7.2 0.0 all-gather.4.cloned.1.call-start
  7.2 0.7 all-gather.4.cloned.1.call-update
  7.9 0.0 all-gather.6.cloned.1.call-start
  7.9 18.0 %all_gather.12 = bf16[1024,256]{1,0:T(8,128)(2,1)S(1)} all-gather(bf16[128,256]{1,0:T(8,128)(2,1)} %param.3), channel_id=1, replica_groups=mesh['rows'=32,'cols'=8] {'cols'}, dimensions={0}, use_global_device_ids=true | all-gather | bytes 589824 | tf_op jit(solution)/shard_map/all_gather | solution.py:10
  25.9 0.2 multiply_reduce_fusion.2
  26.1 96.6 %all-gather.4.cloned.1.call-done = bf16[8192,256]{1,0:T(8,128)(2,1)} async-done(((bf16[256,256]{1,0:T(8,128)(2,1)}), bf16[8192,256]{1,0:T(8,128)(2,1)}) %all-gather.4.cloned.1.call-update) | async-done | bytes 4194320 | tf_op jit(solution)/shard_map/all_gather | solution.py:16
  122.7 3.3 multiply_reduce_fusion.1
  126.0 0.0 copy-start.2
  126.1 15.9 %fusion = (f32[1024]{0:T(1024)S(1)}, f32[1024,8192]{1,0:T(8,128)}) fusion(f32[8192]{0:T(1024)} %param.5, bf16[1024,256]{1,0:T(8,128)(2,1)S(1)} %all_gather.12, bf16[8192,256]{1,0:T(8,128)(2,1)} %all-gather.4.cloned.1.call-done, f32[8192]{0:T(1024)S(1)} %multiply_reduce_fusion.1, f32[1024]{0:T(1024)S(1)} %multiply_reduce_fusion.2), kind=kOutput, calls=%fused_computation.6 | convolution fusion | flops 4353686528 | bytes 38346752 | tf_op jit(solution)/shard_map/dot_general | solution.py:19
  142.0 17.9 %pmax.14 = f32[1024]{0:T(1024)S(1)} all-reduce(f32[1024]{0:T(1024)S(1)} %get-tuple-element.3), channel_id=1, replica_groups=mesh['rows'=32,'cols'=8] {'cols'}, use_global_device_ids=true, to_apply=%region_3.0 | all-reduce | flops 1024 | bytes 8192 | tf_op jit(solution)/shard_map/pmax | solution.py:30
  159.9 0.0 copy-done.2
  159.9 14.7 %exponential_reduce_fusion.1 = f32[1024]{0:T(1024)S(1)} fusion(f32[1024,8192]{1,0:T(8,128)} %get-tuple-element.4, f32[1024]{0:T(1024)S(1)} %get-tuple-element.3, f32[8192]{0:T(1024)S(1)} %copy-done.2), kind=kLoop, calls=%fused_computation.3 | loop fusion | flops 33553408 | bytes 33595392 | tf_op jit(solution)/shard_map/reduce_sum | solution.py:29
  174.7 13.6 %psum.14 = f32[1024]{0:T(1024)S(1)} all-reduce(f32[1024]{0:T(1024)S(1)} %exponential_multiply_fusion), channel_id=1, replica_groups=mesh['rows'=32,'cols'=8] {'cols'}, use_global_device_ids=true, to_apply=%region_5.0 | all-reduce | flops 1024 | bytes 8192 | tf_op jit(solution)/shard_map/psum | solution.py:31
  188.3 0.0 copy-start.1
  188.3 12.9 %fusion.1 = f32[8192]{0:T(1024)S(1)} fusion(f32[1024,8192]{1,0:T(8,128)} %get-tuple-element.4, f32[1024]{0:T(1024)S(1)} %multiply_add_fusion), kind=kLoop, calls=%fused_computation.7 | loop fusion | flops 25157632 | bytes 33591296 | tf_op jit(solution)/shard_map/reduce_max | solution.py:35
  201.2 14.5 %exponential_reduce_fusion = f32[8192]{0:T(1024)S(1)} fusion(f32[1024,8192]{1,0:T(8,128)} %get-tuple-element.4, f32[8192]{0:T(1024)S(1)} %fusion.1, f32[1024]{0:T(1024)S(1)} %multiply_add_fusion), kind=kLoop, calls=%fused_computation.1 | loop fusion | flops 33546240 | bytes 33624064 | tf_op jit(solution)/shard_map/reduce_sum | solution.py:36
  215.7 187.5 %pmax.15 = bf16[8192]{0:T(1024)(128)(2,1)S(1)} all-reduce(bf16[8192]{0:T(1024)(128)(2,1)S(1)} %convert_element_type.14), channel_id=1, replica_groups=mesh['rows'=32,'cols'=8] {'rows'}, use_global_device_ids=true, to_apply=%region_7.0 | all-reduce | flops 8192 | bytes 32768 | tf_op jit(solution)/shard_map/pmax | solution.py:37
  403.2 0.6 fusion.3
  403.9 0.0 all-gather.6.cloned.1.call-update
  403.9 106.2 %all-gather.6.cloned.1.call-done = f32[262144]{0:T(1024)} async-done(((f32[8192]{0:T(1024)}), f32[262144]{0:T(1024)}) %all-gather.6.cloned.1.call-update) | async-done | bytes 1048592 | tf_op jit(solution)/shard_map/all_gather | solution.py:38
  510.1 1.4 reshape.13
  511.5 0.1 reduce_sum.58
  511.6 0.0 copy-done.1
  511.6 0.0 copy-start
  511.7 15.1 %multiply_reduce_fusion = f32[1024]{0:T(1024)S(1)} fusion(f32[1024,8192]{1,0:T(8,128)} %get-tuple-element.4, f32[8192]{0:T(1024)S(1)} %fusion.5, f32[1024]{0:T(1024)S(1)} %multiply_add_fusion), kind=kLoop, calls=%fused_computation | loop fusion | flops 41942016 | bytes 33595392 | tf_op jit(solution)/shard_map/reduce_sum | solution.py:43
  526.7 15.2 %psum.15 = f32[1024]{0:T(1024)S(1)} all-reduce(f32[1024]{0:T(1024)S(1)} %multiply_reduce_fusion), channel_id=1, replica_groups=mesh['rows'=32,'cols'=8] {'cols'}, use_global_device_ids=true, to_apply=%region_11.0 | all-reduce | flops 1024 | bytes 8192 | tf_op jit(solution)/shard_map/psum | solution.py:44
  542.0 0.6 broadcast_multiply_fusion
  542.6 0.0 copy-done
  (4 shorter events, 0.0 us)
Async XLA Ops:
  7.2 115.5 %all-gather.4.cloned.1.call-start = ((), (), s32[]{:S(2)}) async-start(), calls=%async_computation | async-start | bytes 4325376 | tf_op jit(solution)/shard_map/all_gather | solution.py:16
  7.9 502.2 %all-gather.6.cloned.1.call-start = ((), (), s32[]{:S(2)}) async-start(), calls=%async_computation.1 | async-start | bytes 1081344 | tf_op jit(solution)/shard_map/all_gather | solution.py:38
  126.0 33.9 %copy-start.2 = (f32[8192]{0:T(1024)S(1)}, f32[8192]{0:T(1024)}, u32[]{:S(2)}) copy-start(f32[8192]{0:T(1024)} %param.5) | copy-start | bytes 98308
  188.3 323.4 %copy-start.1 = (f32[1024]{0:T(1024)}, f32[1024]{0:T(1024)S(1)}, u32[]{:S(2)}) copy-start(f32[1024]{0:T(1024)S(1)} %multiply_add_fusion) | copy-start | bytes 12292
  511.6 30.9 %copy-start = (f32[8192]{0:T(1024)}, f32[8192]{0:T(1024)S(1)}, u32[]{:S(2)}) copy-start(f32[8192]{0:T(1024)S(1)} %fusion.5) | copy-start | bytes 98308
Sparse Core Ops, SparseCore 0:
  11.4 111.2 all-gather.3
  404.0 106.0 all-gather.5
